TPU v7x, 256 devices: a whole 4x4x8 slice. The times are simulated.
256 devices in a mesh: pair: 32 (over z, y), occ: 8 (over x, core).
Axes of the slice: x: 4, y: 4, z: 8, core: 2. Of those that a mesh axis runs over, the one named last changes fastest.
Arguments:
- amplitudes: float32 [256, 128, 128], P('pair'), may hold values from -4 to 4
- exchange_ints: float32 [256, 128, 128], P('pair'), may hold values from -6 to 6
- pno_energy: float32 [256, 128], P('pair'), may hold values from 0.3 to 3
- pair_shift: float32 [256], P('pair'), may hold values from 0.5 to 2
- coefficients: bfloat16 [256, 512, 128], P('pair'), may hold values from -0.5 to 0.5
- domain_tiles: int32 [256, 4], P('pair'), may hold values from 0 to 3, each once within a row
- couple_owner: int32 [8, 256, 8, 1], P('occ', 'pair'), may hold values from 0 to 31; in each aligned block of 64 rows (0 to 63, 64 to 127, ..., all dimensions but the last counted through in order) at most 3 rows name the same one
- couple_index: int32 [8, 256, 8], P('occ', 'pair'), may hold values from 0 to 7
- couple_weight: float32 [8, 256, 8], P('occ', 'pair'), may hold values from -0.5 to 0.5
Outputs:
- final_amplitudes: float32 [256, 128, 128], P('pair')
- final_residual: float32 [256, 128, 128], P('pair')
Inputs may be any that keep to these rules, and one draw needn't show every extreme that they name: `couple_owner`: among the couplings held by one device (one block of 64 entries), no owner is named more than 3 times. `domain_tiles`: the tiles of one pair's domain are distinct.
All inputs are finite; a program needn't handle non-finite values.
Results may differ from a plain program's by a relative error of at most 0.0003.
Values may be sent and summed in bfloat16 or wider, within the bound.
A program may use at most 128 MiB of HBM per device.

v0:
```python
import jax
import jax.numpy as jnp
from jax import lax
from jax.sharding import Mesh
from jax.sharding import PartitionSpec as P

ITERS = 2
PAIR = ("pair_0", "pair_1")
HIGHEST = lax.Precision.HIGHEST


def in_blocks(x, dim, peers):
    before, after = (x.shape[:dim], x.shape[dim + 1 :])
    return jnp.moveaxis(x.reshape(*before, peers, -1, *after), dim, 0)


def joined_along(pieces, dim):
    lengths = list(pieces.shape[1:])
    lengths[dim] *= pieces.shape[0]
    return jnp.moveaxis(pieces, 0, dim).reshape(lengths)


def moved_by_axis(pieces, axes, order):
    lengths = [lax.axis_size(a) for a in axes]
    pieces = pieces.reshape(*lengths, *pieces.shape[1:])
    for k in order:
        pieces = lax.all_to_all(pieces, axes[k], split_axis=k, concat_axis=k, tiled=True)
    return pieces.reshape(-1, *pieces.shape[len(axes) :])


def stepwise_exchange(x, axes, order, split_dim, concat_dim):
    pieces = in_blocks(x, split_dim, lax.axis_size(axes))
    return joined_along(moved_by_axis(pieces, axes, order), concat_dim)


def over_pieces(x, axis):
    pieces = lax.all_gather(x, axis)
    return pieces.sum(axis=0)


def local(
    amplitudes,
    exchange_ints,
    pno_energy,
    pair_shift,
    coefficients,
    domain_tiles,
    couple_owner,
    couple_index,
    couple_weight,
):
    pair_count = amplitudes.shape[0]
    pno_width = amplitudes.shape[1]
    domain = coefficients.shape[1]
    tile_count = domain_tiles.shape[1]
    couple_count = couple_index.shape[2]
    peer_count = lax.axis_size(PAIR)
    owners = couple_owner.reshape(-1)
    local_index = couple_index.reshape(-1)
    weights = couple_weight.reshape(pair_count, couple_count)
    total_count = owners.shape[0]
    capacity = max(2, 3 * total_count // (2 * peer_count))
    slot_total = peer_count * capacity
    position = jnp.arange(total_count, dtype=jnp.int32)
    same_owner = (owners[:, None] == owners[None, :]) & (position[None, :] < position[:, None])
    slot_rank = jnp.sum(same_owner.astype(jnp.int32), axis=1)
    slot_ids = owners * capacity + slot_rank
    requester_tiles = jnp.repeat(domain_tiles, couple_count, axis=0)
    payload = jnp.concatenate([local_index[:, None], requester_tiles], axis=1)
    requests = jnp.full((slot_total, 1 + tile_count), -1, jnp.int32).at[slot_ids].set(payload)
    arrived = stepwise_exchange(requests, PAIR, (0, 1), 0, 0)
    wanted = arrived[:, 0]
    their_tiles = arrived[:, 1:]
    pick_pair = wanted[:, None] == jnp.arange(pair_count, dtype=jnp.int32)[None, :]
    tile_match = their_tiles[:, :, None, None] == domain_tiles[None, None, :, :]
    selector = (pick_pair[:, None, :, None] & tile_match).astype(jnp.bfloat16)
    selector = selector.reshape(slot_total * tile_count, pair_count * tile_count)
    tile_blocks = coefficients.reshape(pair_count * tile_count, domain // tile_count * pno_width)
    moved_tiles = jnp.dot(selector, tile_blocks, preferred_element_type=jnp.float32).astype(
        jnp.bfloat16
    )
    moved_tiles = moved_tiles.reshape(slot_total, domain, pno_width)
    returned = lax.all_to_all(moved_tiles, PAIR, split_axis=0, concat_axis=0, tiled=True)
    their_coef = jnp.take(returned, slot_ids, axis=0).reshape(
        pair_count, couple_count, domain, pno_width
    )
    intersection = jnp.einsum(
        "pfa,pcfb->pcab", coefficients, their_coef, preferred_element_type=jnp.float32
    )
    denominator = pno_energy[:, :, None] + pno_energy[:, None, :] + pair_shift[:, None, None]
    global_ids = owners * pair_count + local_index
    current = amplitudes
    residual = amplitudes
    for iteration in range(ITERS):
        all_amps = lax.all_gather(current, PAIR, axis=0, tiled=True)
        partner_amp = jnp.take(all_amps, global_ids, axis=0)
        partner_amp = partner_amp.reshape(pair_count, couple_count, pno_width, pno_width)
        inner_prod = jnp.einsum("pcab,pcbd->pcad", intersection, partner_amp, precision=HIGHEST)
        outer_prod = jnp.einsum("pcad,pced->pcae", inner_prod, intersection, precision=HIGHEST)
        partial_value = jnp.einsum("pc,pcae->pae", weights, outer_prod, precision=HIGHEST)
        coupled = over_pieces(partial_value, "occ")
        residual = exchange_ints + denominator * current - coupled
        current = current - residual / denominator
    return (current, residual)


def solution(mesh):
    split = Mesh(mesh.devices.reshape(8, 4, mesh.shape["occ"]), ("pair_0", "pair_1", "occ"))
    in_specs = (
        P(PAIR, None, None),
        P(PAIR, None, None),
        P(PAIR, None),
        P(PAIR),
        P(PAIR, None, None),
        P(PAIR, None),
        P("occ", PAIR, None, None),
        P("occ", PAIR, None),
        P("occ", PAIR, None),
    )
    out_specs = (P(PAIR, None, None), P(PAIR, None, None))
    return jax.shard_map(local, mesh=split, in_specs=in_specs, out_specs=out_specs, check_vma=False)
```

profile of v0, /device:TPU:1, one launch (start us, length us, event | category | flops | bytes accessed | tf_op | source)
XLA Modules:
  0.0 751.8 jit_solution(6762921172561022608)
XLA Ops:
  8.4 1.3 reduce.3
  11.5 0.8 broadcast_in_dim_reshape.2
  13.3 15.9 %all_to_all.15 = s32[8,4,3,5]{3,1,2,0:T(4,128)S(1)} all-to-all(s32[8,4,3,5]{3,1,2,0:T(4,128)S(1)} %copy.36), channel_id=1, replica_groups=mesh['pair_0'=8,'pair_1'=4,'occ'=8] {'pair_0'}, dimensions={0} | all-to-all | bytes 3840 | tf_op jit(solution)/shard_map/all_to_all | solution.py:27
  29.2 0.8 copy.37
  30.0 4.2 all-to-all-start.1
  34.9 1.5 reshape.164
  36.5 2.3 all-to-all-done.1
  39.6 1.3 and.37
  40.9 6.4 convolution_convert_fusion
  47.3 19.6 %reshape.165 = bf16[96,512,128]{2,1,0:T(8,128)(2,1)} reshape(bf16[384,16384]{1,0:T(8,128)(2,1)} %convolution_convert_fusion) | data formatting | bytes 25165824 | tf_op jit(solution)/shard_map/reshape | solution.py:82
  66.9 5.2 all-to-all-start.2
  72.4 351.0 %all-to-all-done.2 = bf16[96,512,128]{2,1,0:T(8,128)(2,1)} async-done(((bf16[96,512,128]{2,1,0:T(8,128)(2,1)}), bf16[96,512,128]{2,1,0:T(8,128)(2,1)}, u32[]{:S(2)}, u32[]{:S(2)}) %all-to-all-start.2) | async-done | bytes 12582944 | tf_op jit(solution)/shard_map/all_to_all | solution.py:83
  423.4 10.2 %gather_fusion = bf16[64,512,128]{2,1,0:T(8,128)(2,1)} fusion(bf16[96,512,128]{2,1,0:T(8,128)(2,1)} %all-to-all-done.2, s32[1024]{0:T(1024)S(1)} %pad_clamp_fusion.1), kind=kCustom, calls=%fused_computation.2 | custom fusion | bytes 16777472 | tf_op jit(solution)/shard_map/jit(_take)/gather | solution.py:84
  433.6 12.2 %copy.41 = bf16[64,512,128]{1,2,0:T(8,128)(2,1)} copy(bf16[64,512,128]{2,1,0:T(8,128)(2,1)} %gather_fusion) | data formatting | bytes 16777216 | tf_op jit(solution)/shard_map/jit(_take)/gather | solution.py:84
  445.8 7.7 %fusion = f32[8,8,128,128]{3,2,1,0:T(8,128)} fusion(bf16[8,8,512,128]{2,3,1,0:T(8,128)(2,1)} %bitcast.63, pred[8,8]{1,0:T(8,128)(4,1)S(1)} %compare_and_fusion.1, bf16[8,512,128]{2,1,0:T(8,128)(2,1)S(1)} %copy-done.6), kind=kOutput, calls=%fused_computation.5 | convolution fusion | flops 1077936128 | bytes 13631552 | tf_op jit(solution)/shard_map/pfa,pcfb->pcab/dot_general | solution.py:87
  453.6 8.5 %gather_fusion.1 = f32[64,128,128]{2,1,0:T(8,128)} fusion(f32[256,128,128]{2,1,0:T(8,128)} %all-gather.7.cloned.1.call-done, s32[1024]{0:T(1024)S(1)} %pad_clamp_fusion), kind=kCustom, calls=%fused_computation.clone | custom fusion | bytes 8388864 | tf_op jit(solution)/shard_map/jit(_take)/gather | solution.py:96
  462.1 2.7 broadcast_select_fusion.1
  465.6 7.3 fusion.14
  472.9 5.8 fusion.15
  478.8 6.1 fusion.5
  484.9 48.7 %all-gather.11.cloned.1.call-done = f32[64,128,128]{2,1,0:T(8,128)} async-done(((f32[8,128,128]{2,1,0:T(8,128)}), f32[64,128,128]{2,1,0:T(8,128)}) %all-gather.11.cloned.1.call-update) | async-done | bytes 4194320 | tf_op jit(solution)/shard_map/all_gather | solution.py:37
  533.6 2.5 reduce_sum.34
  536.1 1.0 divide_subtract_fusion.1
  537.2 139.9 %all-gather.9.cloned.1.call-done = f32[256,128,128]{2,1,0:T(8,128)} async-done(((f32[8,128,128]{2,1,0:T(8,128)}), f32[256,128,128]{2,1,0:T(8,128)}) %all-gather.9.cloned.1.call-update) | async-done | bytes 16777232 | tf_op jit(solution)/shard_map/all_gather | solution.py:95
  677.2 8.5 %gather_fusion.2 = f32[64,128,128]{2,1,0:T(8,128)} fusion(f32[256,128,128]{2,1,0:T(8,128)} %all-gather.9.cloned.1.call-done, s32[1024]{0:T(1024)S(1)} %pad_clamp_fusion), kind=kCustom, calls=%fused_computation.1.clone | custom fusion | bytes 8388864 | tf_op jit(solution)/shard_map/jit(_take)/gather | solution.py:96
  685.7 2.7 broadcast_select_fusion
  689.1 7.3 fusion.16
  696.4 5.9 fusion.17
  702.3 6.1 fusion.3
  708.4 32.6 %all-gather.13.cloned.1.call-done = f32[64,128,128]{2,1,0:T(8,128)} async-done(((f32[8,128,128]{2,1,0:T(8,128)}), f32[64,128,128]{2,1,0:T(8,128)}) %all-gather.13.cloned.1.call-update) | async-done | bytes 4194320 | tf_op jit(solution)/shard_map/all_gather | solution.py:37
  741.1 2.5 reduce_sum.35
  743.6 1.2 divide_subtract_fusion
  (58 shorter events, 7.5 us)
Async XLA Ops:
  7.2 471.5 %copy-start = (f32[1,8,8]{2,1,0:T(8,128)S(1)}, f32[1,8,8]{2,1,0:T(8,128)}, u32[]{:S(2)}) copy-start(f32[1,8,8]{2,1,0:T(8,128)} %param.19) | copy-start | bytes 772
  7.2 446.4 %all-gather.7.cloned.1.call-start = ((), (), s32[]{:S(2)}) async-start(), calls=%async_computation.3 | async-start | bytes 17301504 | tf_op jit(solution)/shard_map/all_gather | solution.py:95
  30.0 8.8 %all-to-all-start.1 = ((s32[8,4,3,5]{0,2,3,1:T(4,128)}), s32[8,4,3,5]{0,2,3,1:T(4,128)S(1)}, u32[]{:S(2)}, u32[]{:S(2)}) async-start(s32[8,4,3,5]{0,2,3,1:T(4,128)} %copy.37), calls=%async_computation.1 | async-start | bytes 81920 | tf_op jit(solution)/shard_map/all_to_all | solution.py:27
  66.9 5.4 copy-start.9
  66.9 5.5 copy-start.8
  66.9 356.5 %all-to-all-start.2 = ((bf16[96,512,128]{2,1,0:T(8,128)(2,1)}), bf16[96,512,128]{2,1,0:T(8,128)(2,1)}, u32[]{:S(2)}, u32[]{:S(2)}) async-start(bf16[96,512,128]{2,1,0:T(8,128)(2,1)} %reshape.165), calls=%async_computation.2 | async-start | bytes 25165824 | tf_op jit(solution)/shard_map/all_to_all | solution.py:83
  72.2 461.4 %all-gather.11.cloned.1.call-start = ((), (), s32[]{:S(2)}) async-start(), calls=%async_computation.5 | async-start | bytes 4718592 | tf_op jit(solution)/shard_map/all_gather | solution.py:37
  433.6 12.2 %copy-start.6 = (bf16[8,512,128]{2,1,0:T(8,128)(2,1)S(1)}, bf16[8,512,128]{2,1,0:T(8,128)(2,1)}, u32[]{:S(2)}) copy-start(bf16[8,512,128]{2,1,0:T(8,128)(2,1)} %param.15) | copy-start | bytes 3145732
  462.1 3.4 copy-start.1
  478.7 57.4 %copy-start.4 = (f32[8,128,128]{2,1,0:T(8,128)S(1)}, f32[8,128,128]{2,1,0:T(8,128)}, u32[]{:S(2)}) copy-start(f32[8,128,128]{2,1,0:T(8,128)} %param.11) | copy-start | bytes 1572868
  478.7 57.4 %copy-start.5 = (f32[8,128,128]{2,1,0:T(8,128)S(1)}, f32[8,128,128]{2,1,0:T(8,128)}, u32[]{:S(2)}) copy-start(f32[8,128,128]{2,1,0:T(8,128)} %param.12) | copy-start | bytes 1572868
  478.7 57.4 %copy-start.7 = (f32[8,128]{1,0:T(8,128)S(1)}, f32[8,128]{1,0:T(8,128)}, u32[]{:S(2)}) copy-start(f32[8,128]{1,0:T(8,128)} %param.13) | copy-start | bytes 12292
  478.7 57.4 %copy-start.10 = (f32[8]{0:T(128)S(1)}, f32[8]{0:T(128)}, u32[]{:S(2)}) copy-start(f32[8]{0:T(128)} %param.14) | copy-start | bytes 100
  484.9 192.3 %all-gather.9.cloned.1.call-start = ((), (), s32[]{:S(2)}) async-start(), calls=%async_computation.4 | async-start | bytes 17301504 | tf_op jit(solution)/shard_map/all_gather | solution.py:95
  537.2 203.9 %all-gather.13.cloned.1.call-start = ((), (), s32[]{:S(2)}) async-start(), calls=%async_computation.6 | async-start | bytes 4718592 | tf_op jit(solution)/shard_map/all_gather | solution.py:37
  685.7 3.4 copy-start.2
  702.3 41.3 %copy-start.3 = (f32[8,128,128]{2,1,0:T(8,128)S(1)}, f32[8,128,128]{2,1,0:T(8,128)}, u32[]{:S(2)}) copy-start(f32[8,128,128]{2,1,0:T(8,128)} %divide_subtract_fusion.1) | copy-start | bytes 1572868
Sparse Core Ops, SparseCore 0:
  10.6 325.4 all-gather.6
  485.0 48.5 all-gather.10
  537.3 139.8 all-gather.8
  708.6 32.4 all-gather.12
where the time goes:
time: 758 us; the launch traced here: 752 us
  waiting for transfers between devices  575 us (76%)
  local copies, waits for them, and re-layouts  68.8 us (9%)
  matrix products  52.6 us (7%)
  blocking collectives  15.9 us (2%)
  other arithmetic  15.2 us (2%)
  between operations  14.5 us (2%)
  starting transfers between devices  9.56 us (1%)
    all_to_all x1, waiting for transfers between devices, local(): lax.all_to_all(moved_tiles, PAIR, split_axis=0, concat_axis=0, tiled=True)  351 us
    all_gather x2, waiting for transfers between devices, local(): all_amps = lax.all_gather(current, PAIR, axis=0, tiled=True)  140 us
    all_gather x2, waiting for transfers between devices, over_pieces(): pieces = lax.all_gather(x, axis)  81.3 us
    gather x2, local copies, waits for them, and re-layouts, local(): jnp.take(returned, slot_ids, axis=0)  22.4 us
    reshape x1, local copies, waits for them, and re-layouts, local(): moved_tiles = moved_tiles.reshape(slot_total, domain, pno_width)  19.6 us
    gather x2, local copies, waits for them, and re-layouts, local(): partner_amp = jnp.take(all_amps, global_ids, axis=0)  17.1 us
    all_to_all x1, blocking collectives, moved_by_axis(): lax.all_to_all(pieces, axes[k], split_axis=k, concat_axis=k, tiled=True)  15.9 us
  transfers between devices with their start and end apart: 6, of which 5 were waited for; matrix products, arithmetic and copies ran while one was open for 9% of the time, Pallas kernels for 0%

commit v1 on v0

--- a/solution.py
+++ b/solution.py
@@ -92,7 +92,9 @@
     current = amplitudes
     residual = amplitudes
     for iteration in range(ITERS):
-        all_amps = lax.all_gather(current, PAIR, axis=0, tiled=True)
+        all_amps = jnp.concatenate(
+            lax.all_to_all(jnp.stack([current] * lax.axis_size(PAIR)), PAIR, 0, 0), axis=0
+        )
         partner_amp = jnp.take(all_amps, global_ids, axis=0)
         partner_amp = partner_amp.reshape(pair_count, couple_count, pno_width, pno_width)
         inner_prod = jnp.einsum("pcab,pcbd->pcad", intersection, partner_amp, precision=HIGHEST)

time: 758 us -> 1270 us (1.68)
  blocking collectives: 15.9 us -> 666 us
  waiting for transfers between devices: 575 us -> 424 us
    all_to_all x0 -> x2, blocking collectives: none -> 650 us  [the longest x1 373 us: local(): lax.all_to_all(jnp.stack([current] * lax.axis_size(PAIR)), PAIR, 0, 0)]
    all_gather x2 -> x0, waiting for transfers between devices: 140 us -> none  [local(): all_amps = lax.all_gather(current, PAIR, axis=0, tiled=True)]
    all_to_all x1, waiting for transfers between devices: 351 us -> 334 us  [local(): lax.all_to_all(jnp.stack([current] * lax.axis_size(PAIR)), PAIR, 0, 0)]
  transfers between devices with their start and end apart: 6 -> 4, of which waited for: 5 -> 4; matrix products, arithmetic and copies ran while one was open for 9% -> 3% of each run, Pallas kernels for 0% -> 0%
where the time goes in v1:
time: 1270 us; the launch traced here: 1260 us
  blocking collectives  666 us (52%)
  waiting for transfers between devices  424 us (33%)
  local copies, waits for them, and re-layouts  78.6 us (6%)
  matrix products  52.5 us (4%)
  between operations  14.8 us (1%)
  other arithmetic  14.4 us (1%)
    all_to_all x1, blocking collectives, local(): lax.all_to_all(jnp.stack([current] * lax.axis_size(PAIR)), PAIR, 0, 0)  373 us
    all_to_all x1, waiting for transfers between devices, local(): lax.all_to_all(jnp.stack([current] * lax.axis_size(PAIR)), PAIR, 0, 0)  334 us
    all_to_all x1, blocking collectives, local(): lax.all_to_all(moved_tiles, PAIR, split_axis=0, concat_axis=0, tiled=True)  276 us
    all_gather x2, waiting for transfers between devices, over_pieces(): pieces = lax.all_gather(x, axis)  87.3 us
  transfers between devices with their start and end apart: 4, of which 4 were waited for; matrix products, arithmetic and copies ran while one was open for 3% of the time, Pallas kernels for 0%

profile of v1, /device:TPU:1, one launch (start us, length us, event | category | flops | bytes accessed | tf_op | source)
XLA Modules:
  0.0 1260.7 jit_solution(2455443069356914828)
XLA Ops:
  8.5 1.3 reduce.3
  12.6 15.9 %all_to_all.25 = s32[8,4,3,5]{3,1,2,0:T(4,128)S(1)} all-to-all(s32[8,4,3,5]{3,1,2,0:T(4,128)S(1)} %copy.36), channel_id=1, replica_groups=mesh['pair_0'=8,'pair_1'=4,'occ'=8] {'pair_0'}, dimensions={0} | all-to-all | bytes 3840 | tf_op jit(solution)/shard_map/all_to_all | solution.py:27
  29.3 4.2 all-to-all-start.1
  34.2 1.5 reshape.174
  35.7 2.1 all-to-all-done.1
  38.6 1.3 and.37
  39.9 6.3 convolution_convert_fusion
  46.2 19.5 %reshape.175 = bf16[96,512,128]{2,1,0:T(8,128)(2,1)} reshape(bf16[384,16384]{1,0:T(8,128)(2,1)} %convolution_convert_fusion) | data formatting | bytes 25165824 | tf_op jit(solution)/shard_map/reshape | solution.py:82
  65.8 276.4 %all_to_all.26 = bf16[96,512,128]{2,1,0:T(8,128)(2,1)} all-to-all(bf16[96,512,128]{2,1,0:T(8,128)(2,1)} %reshape.175), channel_id=1, replica_groups=mesh['pair_0'=8,'pair_1'=4,'occ'=8] {'pair_0','pair_1'}, dimensions={0} | all-to-all | bytes 25165824 | tf_op jit(solution)/shard_map/all_to_all | solution.py:83
  342.1 7.9 stack.4
  350.0 6.9 all-to-all-start.3
  357.2 10.2 gather_fusion
  367.4 12.2 copy.41
  379.6 7.7 fusion
  387.3 334.3 %all-to-all-done.3 = f32[32,8,128,128]{3,2,1,0:T(8,128)} async-done(((f32[32,8,128,128]{3,2,1,0:T(8,128)}), f32[32,8,128,128]{3,2,1,0:T(8,128)}, u32[]{:S(2)}, u32[]{:S(2)}) %all-to-all-start.3) | async-done | bytes 16777248 | tf_op jit(solution)/shard_map/all_to_all | solution.py:96
  721.6 8.5 gather_fusion.1
  730.1 2.7 broadcast_select_fusion.1
  733.6 7.3 fusion.14
  740.8 5.8 fusion.15
  746.7 6.1 fusion.5
  752.9 54.9 %all-gather.5.cloned.1.call-done = f32[64,128,128]{2,1,0:T(8,128)} async-done(((f32[8,128,128]{2,1,0:T(8,128)}), f32[64,128,128]{2,1,0:T(8,128)}) %all-gather.5.cloned.1.call-update) | async-done | bytes 4194320 | tf_op jit(solution)/shard_map/all_gather | solution.py:37
  807.7 2.5 reduce_sum.34
  810.5 2.1 stack.5
  812.6 373.4 %all_to_all.27 = f32[32,8,128,128]{3,2,1,0:T(8,128)} all-to-all(f32[32,8,128,128]{3,2,1,0:T(8,128)S(1)} %stack.5), channel_id=1, replica_groups=mesh['pair_0'=8,'pair_1'=4,'occ'=8] {'pair_0','pair_1'}, dimensions={0} | all-to-all | bytes 33554432 | tf_op jit(solution)/shard_map/all_to_all | solution.py:96
  1186.0 8.5 gather_fusion.2
  1194.6 2.7 broadcast_select_fusion
  1198.0 7.3 fusion.16
  1205.3 5.9 fusion.17
  1211.2 6.1 fusion.3
  1217.3 32.4 %all-gather.7.cloned.1.call-done = f32[64,128,128]{2,1,0:T(8,128)} async-done(((f32[8,128,128]{2,1,0:T(8,128)}), f32[64,128,128]{2,1,0:T(8,128)}) %all-gather.7.cloned.1.call-update) | async-done | bytes 4194320 | tf_op jit(solution)/shard_map/all_gather | solution.py:37
  1249.7 2.5 reduce_sum.35
  1252.2 1.2 divide_subtract_fusion
  (54 shorter events, 8.5 us)
Async XLA Ops:
  7.2 739.5 %copy-start = (f32[1,8,8]{2,1,0:T(8,128)S(1)}, f32[1,8,8]{2,1,0:T(8,128)}, u32[]{:S(2)}) copy-start(f32[1,8,8]{2,1,0:T(8,128)} %param.19) | copy-start | bytes 772
  29.3 8.5 all-to-all-start.1
  65.8 276.4 %copy-start.3 = (f32[8,128,128]{2,1,0:T(8,128)S(1)}, f32[8,128,128]{2,1,0:T(8,128)}, u32[]{:S(2)}) copy-start(f32[8,128,128]{2,1,0:T(8,128)} %param.11) | copy-start | bytes 1572868
  350.0 7.0 copy-start.8
  350.0 7.2 copy-start.7
  350.0 371.6 %all-to-all-start.3 = ((f32[32,8,128,128]{3,2,1,0:T(8,128)}), f32[32,8,128,128]{3,2,1,0:T(8,128)}, u32[]{:S(2)}, u32[]{:S(2)}) async-start(f32[32,8,128,128]{3,2,1,0:T(8,128)} %stack.4), calls=%async_computation.3 | async-start | bytes 33554432 | tf_op jit(solution)/shard_map/all_to_all | solution.py:96
  356.9 450.8 %all-gather.5.cloned.1.call-start = ((), (), s32[]{:S(2)}) async-start(), calls=%async_computation.5 | async-start | bytes 4718592 | tf_op jit(solution)/shard_map/all_gather | solution.py:37
  367.4 12.2 copy-start.5
  730.1 3.4 copy-start.1
  746.7 63.6 %copy-start.4 = (f32[8,128,128]{2,1,0:T(8,128)S(1)}, f32[8,128,128]{2,1,0:T(8,128)}, u32[]{:S(2)}) copy-start(f32[8,128,128]{2,1,0:T(8,128)} %param.12) | copy-start | bytes 1572868
  746.7 63.6 %copy-start.6 = (f32[8,128]{1,0:T(8,128)S(1)}, f32[8,128]{1,0:T(8,128)}, u32[]{:S(2)}) copy-start(f32[8,128]{1,0:T(8,128)} %param.13) | copy-start | bytes 12292
  746.7 63.5 %copy-start.9 = (f32[8]{0:T(128)S(1)}, f32[8]{0:T(128)}, u32[]{:S(2)}) copy-start(f32[8]{0:T(128)} %param.14) | copy-start | bytes 100
  752.8 496.9 %all-gather.7.cloned.1.call-start = ((), (), s32[]{:S(2)}) async-start(), calls=%async_computation.6 | async-start | bytes 4718592 | tf_op jit(solution)/shard_map/all_gather | solution.py:37
  1194.5 3.4 copy-start.2
Sparse Core Ops, SparseCore 0:
  753.0 54.7 all-gather.4
  1217.4 32.2 all-gather.6
